TPU v7x, 32 devices: a whole 2x2x4 slice. The times are simulated.
32 devices in a mesh: groups: 2 (over y), field: 4 (over x, core), wave: 4 (over z).
Axes of the slice: x: 2, y: 2, z: 4, core: 2. Of those that a mesh axis runs over, the one named last changes fastest.
Arguments:
- mode_basis: bfloat16 [22, 512, 512], P(None, 'wave'), may hold values from -6 to 6
- coef_table: bfloat16 [4096, 22], replicated, may hold values from -1.5 to 1.5
- table_index: int32 [64], P(('groups', 'field')), parts along dimension 0, may hold values from 0 to 4095
- wave_lengths: float32 [8], P('wave'), may hold values from 0.32 to 1.05
- sed_table: float32 [1024, 8], replicated, may hold values from 0.05 to 1
- template_ids: int32 [64, 8], P(('groups', 'field')), parts along dimension 0, may hold values from 0 to 1023
Outputs:
- mixed: bfloat16 [64, 8, 256, 256], P(('groups', 'field'), None, 'wave'), parts along dimension 0
There are 2 independent parts, one for each index of `groups`. A program takes and returns all parts, laid end to end along the dimension named above; an argument that names none is the same for every part. Nothing has to cross between parts.
All inputs are finite; a program needn't handle non-finite values.
Results may differ from a plain program's by a relative error of at most 0.0065.
Values may be sent and summed in bfloat16 or wider, within the bound.
A program may use at most 128 MiB of HBM per device.

v0:
```python
import math
import jax
import jax.numpy as jnp
from jax import lax
from jax.sharding import PartitionSpec as P

PUP = 512
PIX = 256
TWO_PI = 2.0 * math.pi
SAMPLING = 0.25
EPSILON = 1e-06


def transform_table(wave_lengths, pixels, pupil_side):
    pixel_offset = jnp.arange(pixels, dtype=jnp.int32) - pixels // 2
    pupil_offset = 2 * jnp.arange(pupil_side, dtype=jnp.int32) - pupil_side + 1
    products = (pixel_offset[:, None] * pupil_offset[None, :]).astype(jnp.float32)
    factor = TWO_PI * SAMPLING / (2.0 * pupil_side) / wave_lengths
    angles = products[None, :, :] * factor[:, None, None]
    cosine = jnp.cos(angles)
    sine_part = jnp.sin(angles)
    upper_half = jnp.concatenate([cosine, sine_part], axis=2)
    lower_half = jnp.concatenate([-sine_part, cosine], axis=2)
    return jnp.concatenate([upper_half, lower_half], axis=1).astype(jnp.bfloat16)


def aperture_rows(row_start, row_count, pupil_side):
    row_pos = 2 * (row_start + jnp.arange(row_count, dtype=jnp.int32)) - pupil_side + 1
    col_pos = 2 * jnp.arange(pupil_side, dtype=jnp.int32) - pupil_side + 1
    radius_sq = row_pos[:, None] * row_pos[:, None] + col_pos[None, :] * col_pos[None, :]
    inner_edge = 61 * pupil_side // 100
    inside = (radius_sq <= pupil_side * pupil_side) & (radius_sq >= inner_edge * inner_edge)
    return inside.astype(jnp.float32)


def pupil_section(path_rows, wave_lengths, kernel_table, row_start):
    row_count = path_rows.shape[1]
    pupil_side = path_rows.shape[2]
    opening = aperture_rows(row_start, row_count, pupil_side)
    phase_map = path_rows[:, None, :, :] * (TWO_PI / wave_lengths)[None, :, None, None]
    field_real = opening * jnp.cos(phase_map)
    field_imag = opening * jnp.sin(phase_map)
    pupil_field = jnp.concatenate([field_real, field_imag], axis=3).astype(jnp.bfloat16)
    first_pass = jnp.einsum(
        "flxy,luy->flxu", pupil_field, kernel_table, preferred_element_type=jnp.float32
    )
    return first_pass.astype(jnp.bfloat16)


def finish_section(first_pass, kernel_table):
    pixels = first_pass.shape[3] // 2
    stacked = jnp.concatenate([first_pass[..., :pixels], first_pass[..., pixels:]], axis=2)
    image_field = jnp.einsum(
        "lux,flxv->fluv", kernel_table, stacked, preferred_element_type=jnp.float32
    )
    intensity = (
        image_field[:, :, :pixels] * image_field[:, :, :pixels]
        + image_field[:, :, pixels:] * image_field[:, :, pixels:]
    )
    mean_level = jnp.mean(intensity, axis=(2, 3), keepdims=True)
    return (intensity / (mean_level + EPSILON)).astype(jnp.bfloat16)


def local(mode_basis, coef_table, table_index, wave_lengths, sed_table, template_ids):
    kernel_table = transform_table(wave_lengths, PIX, PUP)
    table_rows = coef_table.shape[0]
    selector = (table_index[:, None] == jnp.arange(table_rows, dtype=jnp.int32)[None, :]).astype(
        jnp.bfloat16
    )
    coeffs = jnp.dot(selector, coef_table, preferred_element_type=jnp.float32).astype(jnp.bfloat16)
    mode_count = mode_basis.shape[0]
    positions = coeffs.shape[0]
    whole_basis = lax.all_gather(mode_basis, "wave", axis=1, tiled=True)
    path_diff = jnp.dot(
        coeffs, whole_basis.reshape(mode_count, -1), preferred_element_type=jnp.float32
    )
    path_diff = path_diff.reshape(positions, PUP, PUP)
    first_pass = pupil_section(path_diff, wave_lengths, kernel_table, 0)
    spectra = finish_section(first_pass, kernel_table)
    pixel_slabs = lax.all_to_all(spectra, "wave", split_axis=2, concat_axis=1, tiled=True)
    sed_rows = sed_table.shape[0]
    one_hot = (
        template_ids[:, :, None] == jnp.arange(sed_rows, dtype=jnp.int32)[None, None, :]
    ).astype(jnp.float32)
    raw_weights = jnp.einsum("fjn,nl->fjl", one_hot, sed_table, precision=lax.Precision.HIGHEST)
    weights = (raw_weights / jnp.sum(raw_weights, axis=2, keepdims=True)).astype(jnp.bfloat16)
    mixed = jnp.einsum("fjl,flrp->fjrp", weights, pixel_slabs, preferred_element_type=jnp.float32)
    return mixed.astype(jnp.bfloat16)


def solution(mesh):
    return jax.shard_map(
        local,
        mesh=mesh,
        in_specs=(
            P(None, "wave", None),
            P(),
            P(("groups", "field")),
            P("wave"),
            P(),
            P(("groups", "field"), None),
        ),
        out_specs=P(("groups", "field"), None, "wave", None),
        check_vma=False,
    )
```

profile of v0, /device:TPU:0, one launch (start us, length us, event | category | flops | bytes accessed | tf_op | source)
XLA Modules:
  0.0 431.0 jit_solution(3552195632405545953)
XLA Ops:
  6.5 0.7 all-gather.2.cloned.1.call-update
  7.3 0.7 broadcast_divide_fusion.1
  8.0 0.1 multiply_convert_fusion
  8.1 0.2 fusion.30
  8.3 4.1 fusion.22
  12.4 200.3 %all-gather.2.cloned.1.call-done = bf16[22,512,512]{2,1,0:T(8,128)(2,1)} async-done(((bf16[22,128,512]{2,1,0:T(8,128)(2,1)}), bf16[22,512,512]{2,1,0:T(8,128)(2,1)}) %all-gather.2.cloned.1.call-update) | async-done | bytes 11534352 | tf_op jit(solution)/shard_map/all_gather | solution.py:73
  212.7 10.0 %slice_bitcast_fusion = bf16[512,512,22]{1,0,2:T(8,128)(2,1)} fusion(bf16[22,512,512]{2,1,0:T(8,128)(2,1)} %all-gather.2.cloned.1.call-done), kind=kLoop, calls=%fused_computation.13 | loop fusion | bytes 23068672 | tf_op jit(solution)/shard_map/reshape.39
  222.7 24.2 %fusion.9 = f32[8,512,512]{2,0,1:T(8,128)} fusion(bf16[512,512,22]{1,0,2:T(8,128)(2,1)} %slice_bitcast_fusion, bf16[4096,22]{0,1:T(8,128)(2,1)S(1)} %copy-done, s32[8]{0:T(128)S(1)} %copy-done.3), kind=kOutput, calls=%fused_computation.11 | convolution fusion | flops 93749424 | bytes 20103200 | tf_op jit(solution)/shard_map/dot_general | solution.py:74
  247.0 8.2 %copy.20 = f32[8,512,512]{2,1,0:T(8,128)S(1)} copy(f32[8,512,512]{2,0,1:T(8,128)} %fusion.9) | data formatting | bytes 16777216 | tf_op jit(solution)/shard_map/dot_general | solution.py:74
  255.2 64.3 %fusion.2 = (bf16[8,2,512,512]{3,2,0,1:T(8,128)(2,1)}, bf16[8,2,512,512]{3,2,0,1:T(8,128)(2,1)}) fusion(f32[2]{0:T(128)S(1)} %get-tuple-element.13, f32[8,512,512]{2,1,0:T(8,128)S(1)} %copy.20, f32[512,512]{1,0:T(8,128)S(1)} %fusion.30), kind=kLoop, calls=%fused_computation.4 | loop fusion | flops 20971520 | bytes 26214408 | tf_op jit(solution)/shard_map/convert
  319.5 14.6 %convert_bitcast_fusion = bf16[8,2,512,512]{3,2,0,1:T(8,128)(2,1)} fusion(bf16[8,2,512,512]{3,2,0,1:T(8,128)(2,1)} %get-tuple-element.6, bf16[8,2,512,512]{3,2,0,1:T(8,128)(2,1)} %get-tuple-element.5, bf16[2,256,512]{2,1,0:T(8,128)(2,1)S(1)} %get-tuple-element.11, bf16[2,256,512]{2,1,0:T(8,128)(2,1)S(1)} %get-tuple-element.10, ...), kind=kOutput, calls=%fused_computation.18 | convolution fusion | flops 8636071936 | bytes 26738688 | tf_op jit(solution)/shard_map/flxy,luy->flxu/dot_general | solution.py:44
  334.1 5.8 %fusion.41 = (bf16[8,2,512,256]{3,2,0,1:T(8,128)(2,1)}, bf16[8,2,512,256]{3,2,0,1:T(8,128)(2,1)}) fusion(bf16[8,2,512,512]{3,2,0,1:T(8,128)(2,1)} %convert_bitcast_fusion), kind=kLoop, calls=%fused_computation.58 | loop fusion | bytes 16777216 | tf_op jit(solution)/shard_map/slice | solution.py:52
  339.9 11.0 %fusion.18 = f32[8,2,512,256]{2,3,0,1:T(8,128)} fusion(bf16[8,2,512,256]{3,2,0,1:T(8,128)(2,1)} %get-tuple-element.8, bf16[8,2,512,256]{3,2,0,1:T(8,128)(2,1)} %get-tuple-element.7, bf16[2,256,512]{2,1,0:T(8,128)(2,1)S(1)} %get-tuple-element.11, bf16[2,256,512]{2,1,0:T(8,128)(2,1)S(1)} %get-tuple-element.10, bf16[2,256,512]{2,1,0:T(8,128)(2,1)S(1)} %get-tuple-element.9), kind=kOutput, calls=%fused_computation.23 | convolution fusion | flops 4320133120 | bytes 18350080 | tf_op jit(solution)/shard_map/lux,flxv->fluv/dot_general | solution.py:53
  351.0 4.3 fusion.31
  355.3 1.6 copy-done.2
  356.8 0.8 divide_convert_fusion
  357.6 3.1 copy.22
  360.7 3.6 all-to-all-start
  364.3 1.0 fusion.32
  365.4 47.6 %all-to-all-done = bf16[8,2,256,256]{3,0,1,2:T(8,128)(2,1)S(1)} async-done(((bf16[8,2,256,256]{3,0,1,2:T(8,128)(2,1)}), bf16[8,2,256,256]{3,0,1,2:T(8,128)(2,1)S(1)}, u32[]{:S(2)}, u32[]{:S(2)}) %all-to-all-start) | async-done | bytes 2097184 | tf_op jit(solution)/shard_map/all_to_all | solution.py:80
  413.0 2.9 copy.24
  415.9 2.8 all_to_all.16
  418.7 2.0 convolution_convert_fusion
  420.7 3.5 copy.26
  (16 shorter events, 0.1 us)
Async XLA Ops:
  6.5 216.2 %copy-start = (bf16[4096,22]{0,1:T(8,128)(2,1)S(1)}, bf16[4096,22]{0,1:T(8,128)(2,1)}, u32[]{:S(2)}) copy-start(bf16[4096,22]{0,1:T(8,128)(2,1)} %param.7) | copy-start | bytes 540676
  6.5 206.2 %all-gather.2.cloned.1.call-start = ((), (), s32[]{:S(2)}) async-start(), calls=%async_computation.1 | async-start | bytes 14417920 | tf_op jit(solution)/shard_map/all_gather | solution.py:73
  12.4 210.3 %copy-start.3 = (s32[8]{0:T(128)S(1)}, s32[8]{0:T(128)}, u32[]{:S(2)}) copy-start(s32[8]{0:T(128)} %param.8) | copy-start | bytes 100
  351.0 5.8 %copy-start.2 = (f32[8,2,512,256]{2,3,0,1:T(8,128)S(1)}, f32[8,2,512,256]{2,3,0,1:T(8,128)}, u32[]{:S(2)}) copy-start(f32[8,2,512,256]{2,3,0,1:T(8,128)} %fusion.18) | copy-start | bytes 25165828
  357.6 6.7 %copy-start.4 = (f32[1024,8]{0,1:T(8,128)S(1)}, f32[1024,8]{0,1:T(8,128)}, u32[]{:S(2)}) copy-start(f32[1024,8]{0,1:T(8,128)} %param.10) | copy-start | bytes 98308
  357.6 6.7 %copy-start.5 = (s32[8,8]{1,0:T(8,128)S(1)}, s32[8,8]{1,0:T(8,128)}, u32[]{:S(2)}) copy-start(s32[8,8]{1,0:T(8,128)} %param.11) | copy-start | bytes 772
  360.7 52.3 %all-to-all-start = ((bf16[8,2,256,256]{3,0,1,2:T(8,128)(2,1)}), bf16[8,2,256,256]{3,0,1,2:T(8,128)(2,1)S(1)}, u32[]{:S(2)}, u32[]{:S(2)}) async-start(bf16[8,2,256,256]{3,0,1,2:T(8,128)(2,1)} %copy.22), calls=%async_computation | async-start | bytes 4194304 | tf_op jit(solution)/shard_map/all_to_all | solution.py:80
  415.9 8.3 %copy-start.1 = (bf16[4096,22]{0,1:T(8,128)(2,1)S(1)}, bf16[4096,22]{0,1:T(8,128)(2,1)}, u32[]{:S(2)}) copy-start(bf16[4096,22]{0,1:T(8,128)(2,1)} %param.7) | copy-start | bytes 540676
Sparse Core Ops, SparseCore 0:
  8.9 203.7 all-gather.1
where the time goes:
time: 431 us
  waiting for transfers between devices  249 us (58%)
  other arithmetic  74.5 us (17%)
  matrix products  52.9 us (12%)
  local copies, waits for them, and re-layouts  37.8 us (9%)
  between operations  13.5 us (3%)
    all_gather x1, waiting for transfers between devices, local(): whole_basis = lax.all_gather(mode_basis, 'wave', axis=1, tiled=True)  200 us
    another operation x2, other arithmetic  68.4 us
    all_to_all x1, waiting for transfers between devices, local(): lax.all_to_all(spectra, 'wave', split_axis=2, concat_axis=1, tiled=True)  47.6 us
    dot_general x1, matrix products, local(): jnp.dot(coeffs, whole_basis.reshape(mode_count, -1), preferred_element_ty...  24.2 us
    dot_general x1, matrix products, pupil_section(): jnp.einsum('flxy,luy->flxu', pupil_field, kernel_table, preferred_element...  14.6 us
    dot_general x1, matrix products, finish_section(): jnp.einsum('lux,flxv->fluv', kernel_table, stacked, preferred_element_typ...  11 us
    another operation x1, local copies, waits for them, and re-layouts  9.99 us
  transfers between devices with their start and end apart: 2, of which 2 were waited for; matrix products, arithmetic and copies ran while one was open for 1% of the time, Pallas kernels for 0%

commit v1 on v0

--- a/solution.py
+++ b/solution.py
@@ -9,6 +9,22 @@
 TWO_PI = 2.0 * math.pi
 SAMPLING = 0.25
 EPSILON = 1e-06
+
+
+def carry_threads(block_here, axis_tag, dim_k):
+    axis_n = lax.axis_size(axis_tag)
+    frames = [block_here]
+    for dev_j in tuple(range(axis_n - 1)):
+        frames.append(
+            lax.ppermute(
+                frames[-1], axis_name=axis_tag, perm=[(i, (i + 1) % axis_n) for i in range(axis_n)]
+            )
+        )
+    return jnp.roll(
+        jnp.concatenate(frames[::-1], axis=dim_k),
+        (lax.axis_index(axis_tag) + 1) * block_here.shape[dim_k],
+        axis=dim_k,
+    )
 
 
 def transform_table(wave_lengths, pixels, pupil_side):
@@ -70,7 +86,7 @@
     coeffs = jnp.dot(selector, coef_table, preferred_element_type=jnp.float32).astype(jnp.bfloat16)
     mode_count = mode_basis.shape[0]
     positions = coeffs.shape[0]
-    whole_basis = lax.all_gather(mode_basis, "wave", axis=1, tiled=True)
+    whole_basis = carry_threads(mode_basis, "wave", 1)
     path_diff = jnp.dot(
         coeffs, whole_basis.reshape(mode_count, -1), preferred_element_type=jnp.float32
     )

time: 431 us -> 414 us (0.961)
  waiting for transfers between devices: 249 us -> 233 us
  between operations: 13.5 us -> 0.21 us
  local copies, waits for them, and re-layouts: 37.8 us -> 43.8 us
    all_gather x1 -> x0, waiting for transfers between devices: 200 us -> none  [local(): whole_basis = lax.all_gather(mode_basis, 'wave', axis=1, tiled=True)]
    ppermute x0 -> x3, waiting for transfers between devices: none -> 188 us  [carry_threads(): lax.ppermute(frames[-1], axis_name=axis_tag, perm=[(i, (i + 1) % axis_n)...]
    unnamed x12 -> x29, local copies, waits for them, and re-layouts: 1.58 us -> 10.7 us
    another operation x1, local copies, waits for them, and re-layouts: 9.99 us -> 5.19 us
  transfers between devices with their start and end apart: 2 -> 4, of which waited for: 2 -> 4; matrix products, arithmetic and copies ran while one was open for 1% -> 2% of each run, Pallas kernels for 0% -> 0%
where the time goes in v1:
time: 414 us; the launch traced here: 413 us
  waiting for transfers between devices  233 us (56%)
  other arithmetic  76.2 us (18%)
  matrix products  53.2 us (13%)
  local copies, waits for them, and re-layouts  43.8 us (11%)
  starting transfers between devices  6.64 us (2%)
    ppermute x3, waiting for transfers between devices, carry_threads(): lax.ppermute(frames[-1], axis_name=axis_tag, perm=[(i, (i + 1) % axis_n)...  188 us
    another operation x2, other arithmetic  69.2 us
    all_to_all x1, waiting for transfers between devices, local(): lax.all_to_all(spectra, 'wave', split_axis=2, concat_axis=1, tiled=True)  45 us
    dot_general x1, matrix products, local(): jnp.dot(coeffs, whole_basis.reshape(mode_count, -1), preferred_element_ty...  24.4 us
    dot_general x1, matrix products, pupil_section(): jnp.einsum('flxy,luy->flxu', pupil_field, kernel_table, preferred_element...  14.6 us
    dot_general x1, matrix products, finish_section(): jnp.einsum('lux,flxv->fluv', kernel_table, stacked, preferred_element_typ...  11 us
    unnamed x29, local copies, waits for them, and re-layouts  10.7 us
    dot_general x1, local copies, waits for them, and re-layouts, local(): jnp.dot(coeffs, whole_basis.reshape(mode_count, -1), preferred_element_ty...  8.33 us
  transfers between devices with their start and end apart: 4, of which 4 were waited for; matrix products, arithmetic and copies ran while one was open for 2% of the time, Pallas kernels for 0%

profile of v1, /device:TPU:0, one launch (start us, length us, event | category | flops | bytes accessed | tf_op | source)
XLA Modules:
  0.0 413.3 jit_solution(9372185193297792236)
XLA Ops:
  0.0 3.0 collective-permute-start
  3.0 64.7 %collective-permute-done = bf16[22,128,512]{2,1,0:T(8,128)(2,1)S(1)} collective-permute-done((bf16[22,128,512]{2,1,0:T(8,128)(2,1)}, bf16[22,128,512]{2,1,0:T(8,128)(2,1)S(1)}, u32[]{:S(2)}, u32[]{:S(2)}) %collective-permute-start) | collective-permute-done | bytes 2883616 | tf_op jit(solution)/shard_map/ppermute | solution.py:19
  67.7 65.6 %collective-permute-done.1 = bf16[22,128,512]{2,1,0:T(8,128)(2,1)} collective-permute-done((bf16[22,128,512]{2,1,0:T(8,128)(2,1)S(1)}, bf16[22,128,512]{2,1,0:T(8,128)(2,1)}, u32[]{:S(2)}, u32[]{:S(2)}) %collective-permute-start.1) | collective-permute-done | bytes 2883616 | tf_op jit(solution)/shard_map/ppermute | solution.py:19
  135.3 4.9 %fusion.22 = (bf16[2,256,512]{2,1,0:T(8,128)(2,1)}, bf16[2,256,512]{2,1,0:T(8,128)(2,1)}, bf16[2,256,512]{2,1,0:T(8,128)(2,1)}) fusion(f32[2]{0:T(128)S(1)} %get-tuple-element.12, f32[256,512]{1,0:T(8,128)S(1)} %multiply_convert_fusion), kind=kLoop, calls=%fused_computation.31 | loop fusion | flops 1310720 | bytes 2097160 | tf_op jit(solution)/shard_map/convert.7
  140.2 58.0 %collective-permute-done.2 = bf16[22,128,512]{2,1,0:T(8,128)(2,1)} collective-permute-done((bf16[22,128,512]{2,1,0:T(8,128)(2,1)}, bf16[22,128,512]{2,1,0:T(8,128)(2,1)}, u32[]{:S(2)}, u32[]{:S(2)}) %collective-permute-start.2) | collective-permute-done | bytes 2883616 | tf_op jit(solution)/shard_map/ppermute | solution.py:19
  198.2 2.1 constant_dynamic-update-slice_fusion.7
  200.2 2.1 constant_dynamic-update-slice_fusion.6
  202.9 2.1 constant_dynamic-update-slice_fusion.3
  205.0 2.1 constant_dynamic-update-slice_fusion.2
  208.9 5.2 %slice_bitcast_fusion = bf16[512,512,22]{1,0,2:T(8,128)(2,1)} fusion(bf16[22,512,512]{2,1,0:T(8,128)(2,1)S(1)} %constant_dynamic-slice_fusion), kind=kLoop, calls=%fused_computation.13 | loop fusion | bytes 23068672 | tf_op jit(solution)/shard_map/reshape.39
  214.1 24.4 %fusion.9 = f32[8,512,512]{2,0,1:T(8,128)} fusion(bf16[512,512,22]{1,0,2:T(8,128)(2,1)} %slice_bitcast_fusion, bf16[4096,22]{0,1:T(8,128)(2,1)S(1)} %copy-done, s32[8]{0:T(128)S(1)} %copy-done.8), kind=kOutput, calls=%fused_computation.11 | convolution fusion | flops 93749424 | bytes 20103200 | tf_op jit(solution)/shard_map/dot_general | solution.py:90
  238.5 8.3 %copy.20 = f32[8,512,512]{2,1,0:T(8,128)S(1)} copy(f32[8,512,512]{2,0,1:T(8,128)} %fusion.9) | data formatting | bytes 16777216 | tf_op jit(solution)/shard_map/dot_general | solution.py:90
  246.9 64.3 %fusion.2 = (bf16[8,2,512,512]{3,2,0,1:T(8,128)(2,1)}, bf16[8,2,512,512]{3,2,0,1:T(8,128)(2,1)}) fusion(f32[2]{0:T(128)S(1)} %get-tuple-element.13, f32[8,512,512]{2,1,0:T(8,128)S(1)} %copy.20, f32[512,512]{1,0:T(8,128)S(1)} %copy-done.4), kind=kLoop, calls=%fused_computation.4 | loop fusion | flops 20971520 | bytes 26214408 | tf_op jit(solution)/shard_map/convert
  311.3 14.6 %convert_bitcast_fusion = bf16[8,2,512,512]{3,2,0,1:T(8,128)(2,1)} fusion(bf16[8,2,512,512]{3,2,0,1:T(8,128)(2,1)} %get-tuple-element.6, bf16[8,2,512,512]{3,2,0,1:T(8,128)(2,1)} %get-tuple-element.5, bf16[2,256,512]{2,1,0:T(8,128)(2,1)S(1)} %copy-done.7, bf16[2,256,512]{2,1,0:T(8,128)(2,1)S(1)} %copy-done.6, bf16[2,256,512]{2,1,0:T(8,128)(2,1)S(1)} %copy-done.5), kind=kOutput, calls=%fused_computation.18 | convolution fusion | flops 8636071936 | bytes 26738688 | tf_op jit(solution)/shard_map/flxy,luy->flxu/dot_general | solution.py:60
  325.9 5.8 %fusion.41 = (bf16[8,2,512,256]{3,2,0,1:T(8,128)(2,1)}, bf16[8,2,512,256]{3,2,0,1:T(8,128)(2,1)}) fusion(bf16[8,2,512,512]{3,2,0,1:T(8,128)(2,1)} %convert_bitcast_fusion), kind=kLoop, calls=%fused_computation.67 | loop fusion | bytes 16777216 | tf_op jit(solution)/shard_map/slice | solution.py:68
  331.7 11.0 %fusion.18 = f32[8,2,512,256]{2,3,0,1:T(8,128)} fusion(bf16[8,2,512,256]{3,2,0,1:T(8,128)(2,1)} %get-tuple-element.8, bf16[8,2,512,256]{3,2,0,1:T(8,128)(2,1)} %get-tuple-element.7, bf16[2,256,512]{2,1,0:T(8,128)(2,1)S(1)} %copy-done.7, bf16[2,256,512]{2,1,0:T(8,128)(2,1)S(1)} %copy-done.6, bf16[2,256,512]{2,1,0:T(8,128)(2,1)S(1)} %copy-done.5), kind=kOutput, calls=%fused_computation.23 | convolution fusion | flops 4320133120 | bytes 18350080 | tf_op jit(solution)/shard_map/lux,flxv->fluv/dot_general | solution.py:69
  342.7 4.3 %fusion.31 = f32[8,2]{0,1:T(2,128)S(1)} fusion(f32[8,2,512,256]{2,3,0,1:T(8,128)} %fusion.18), kind=kLoop, calls=%fused_computation.41 | loop fusion | flops 4194288 | bytes 8388672 | tf_op jit(solution)/shard_map/reduce_sum | solution.py:76
  349.3 3.1 copy.22
  352.4 3.6 all-to-all-start
  357.1 45.0 %all-to-all-done = bf16[8,2,256,256]{3,0,1,2:T(8,128)(2,1)S(1)} async-done(((bf16[8,2,256,256]{3,0,1,2:T(8,128)(2,1)}), bf16[8,2,256,256]{3,0,1,2:T(8,128)(2,1)S(1)}, u32[]{:S(2)}, u32[]{:S(2)}) %all-to-all-start) | async-done | bytes 2097184 | tf_op jit(solution)/shard_map/all_to_all | solution.py:96
  402.1 2.9 copy.24
  405.0 2.7 all_to_all.16
  407.8 2.1 convolution_convert_fusion
  409.9 3.5 copy.26
  (38 shorter events, 7.8 us)
Async XLA Ops:
  0.0 214.1 %copy-start = (bf16[4096,22]{0,1:T(8,128)(2,1)S(1)}, bf16[4096,22]{0,1:T(8,128)(2,1)}, u32[]{:S(2)}) copy-start(bf16[4096,22]{0,1:T(8,128)(2,1)} %param.7) | copy-start | bytes 540676
  0.0 67.7 %collective-permute-start = (bf16[22,128,512]{2,1,0:T(8,128)(2,1)}, bf16[22,128,512]{2,1,0:T(8,128)(2,1)S(1)}, u32[]{:S(2)}, u32[]{:S(2)}) collective-permute-start(bf16[22,128,512]{2,1,0:T(8,128)(2,1)} %param.6), channel_id=1, source_target_pairs={{0,1},{1,2},{2,3},{3,0},{4,5},{5,6},{6,7},{7,4},{8,9},{9,10},{10,1... | collective-permute-start | bytes 8650760 | tf_op jit(solution)/shard_map/ppermute | solution.py:19
  67.7 65.6 %collective-permute-start.1 = (bf16[22,128,512]{2,1,0:T(8,128)(2,1)S(1)}, bf16[22,128,512]{2,1,0:T(8,128)(2,1)}, u32[]{:S(2)}, u32[]{:S(2)}) collective-permute-start(bf16[22,128,512]{2,1,0:T(8,128)(2,1)S(1)} %collective-permute-done), channel_id=1, source_target_pairs={{0,1},{1,2},{2,3},{3,0},{4,5},{5,6},{6,7},{7,4},{8,9},{9,10},{10,1... | collective-permute-start | bytes 8650760 | tf_op jit(solution)/shard_map/ppermute | solution.py:19
  133.3 64.9 %collective-permute-start.2 = (bf16[22,128,512]{2,1,0:T(8,128)(2,1)}, bf16[22,128,512]{2,1,0:T(8,128)(2,1)}, u32[]{:S(2)}, u32[]{:S(2)}) collective-permute-start(bf16[22,128,512]{2,1,0:T(8,128)(2,1)} %collective-permute-done.1), channel_id=1, source_target_pairs={{0,1},{1,2},{2,3},{3,0},{4,5},{5,6},{6,7},{7,4},{8,9},{9,10},{10,1... | collective-permute-start | bytes 8650760 | tf_op jit(solution)/shard_map/ppermute | solution.py:19
  140.2 62.4 %copy-start.3 = (bf16[22,128,512]{2,1,0:T(8,128)(2,1)S(1)}, bf16[22,128,512]{2,1,0:T(8,128)(2,1)}, u32[]{:S(2)}) copy-start(bf16[22,128,512]{2,1,0:T(8,128)(2,1)} %param.6) | copy-start | bytes 8650756
  208.9 5.2 %copy-start.8 = (s32[8]{0:T(128)S(1)}, s32[8]{0:T(128)}, u32[]{:S(2)}) copy-start(s32[8]{0:T(128)} %param.8) | copy-start | bytes 100
  238.5 8.3 %copy-start.4 = (f32[512,512]{1,0:T(8,128)S(1)}, f32[512,512]{1,0:T(8,128)}, u32[]{:S(2)}) copy-start(f32[512,512]{1,0:T(8,128)} %fusion.30) | copy-start | bytes 3145732
  246.9 64.4 %copy-start.5 = (bf16[2,256,512]{2,1,0:T(8,128)(2,1)S(1)}, bf16[2,256,512]{2,1,0:T(8,128)(2,1)}, u32[]{:S(2)}) copy-start(bf16[2,256,512]{2,1,0:T(8,128)(2,1)} %get-tuple-element.9) | copy-start | bytes 1572868
  246.9 64.4 %copy-start.6 = (bf16[2,256,512]{2,1,0:T(8,128)(2,1)S(1)}, bf16[2,256,512]{2,1,0:T(8,128)(2,1)}, u32[]{:S(2)}) copy-start(bf16[2,256,512]{2,1,0:T(8,128)(2,1)} %get-tuple-element.10) | copy-start | bytes 1572868
  246.9 64.4 %copy-start.7 = (bf16[2,256,512]{2,1,0:T(8,128)(2,1)S(1)}, bf16[2,256,512]{2,1,0:T(8,128)(2,1)}, u32[]{:S(2)}) copy-start(bf16[2,256,512]{2,1,0:T(8,128)(2,1)} %get-tuple-element.11) | copy-start | bytes 1572868
  342.7 5.8 %copy-start.2 = (f32[8,2,512,256]{2,3,0,1:T(8,128)S(1)}, f32[8,2,512,256]{2,3,0,1:T(8,128)}, u32[]{:S(2)}) copy-start(f32[8,2,512,256]{2,3,0,1:T(8,128)} %fusion.18) | copy-start | bytes 25165828
  348.5 7.5 %copy-start.9 = (f32[1024,8]{0,1:T(8,128)S(1)}, f32[1024,8]{0,1:T(8,128)}, u32[]{:S(2)}) copy-start(f32[1024,8]{0,1:T(8,128)} %param.10) | copy-start | bytes 98308
  348.5 7.5 %copy-start.10 = (s32[8,8]{1,0:T(8,128)S(1)}, s32[8,8]{1,0:T(8,128)}, u32[]{:S(2)}) copy-start(s32[8,8]{1,0:T(8,128)} %param.11) | copy-start | bytes 772
  352.4 49.7 %all-to-all-start = ((bf16[8,2,256,256]{3,0,1,2:T(8,128)(2,1)}), bf16[8,2,256,256]{3,0,1,2:T(8,128)(2,1)S(1)}, u32[]{:S(2)}, u32[]{:S(2)}) async-start(bf16[8,2,256,256]{3,0,1,2:T(8,128)(2,1)} %copy.22), calls=%async_computation | async-start | bytes 4194304 | tf_op jit(solution)/shard_map/all_to_all | solution.py:96
  402.1 11.3 %copy-start.1 = (bf16[4096,22]{0,1:T(8,128)(2,1)S(1)}, bf16[4096,22]{0,1:T(8,128)(2,1)}, u32[]{:S(2)}) copy-start(bf16[4096,22]{0,1:T(8,128)(2,1)} %param.7) | copy-start | bytes 540676
